TPU v7x, 32 devices: a whole 2x2x4 slice. The times are simulated.
32 devices in a mesh: rcpt: 16 (over z, y, core), lon: 2 (over x).
Axes of the slice: x: 2, y: 2, z: 4, core: 2. Of those that a mesh axis runs over, the one named last changes fastest.
Arguments:
- adjoint_in: float32 [16, 4, 32, 16, 128], P('rcpt', None, 'lon'), may hold values from -6 to 6
- courants: float32 [16, 3, 32, 16, 128], P('rcpt', None, 'lon'), may hold values from -0.45 to 0.45
- owner: int32 [2], P('lon'), may hold values from 0 to 15
- rcpt_cell: int32 [16, 512], P('rcpt'), may hold values from 0 to 65535
- rcpt_hour: int32 [16, 512], P('rcpt'), may hold values from 0 to 2
- forcing: float32 [16, 4, 512], P('rcpt'), may hold values from -24 to 24
Outputs:
- adjoint_out: float32 [16, 4, 32, 16, 128], P('rcpt', None, 'lon')
Inputs may be any that keep to these rules, and one draw needn't show every extreme that they name: `owner`: each band's met is read from one receptor row's slot. `rcpt_cell`: flat index (longitude * 16 + level) * 128 + latitude; several receptors may share a cell.
All inputs are finite; a program needn't handle non-finite values.
Results may differ from a plain program's by a relative error of at most 0.0003.
Values sent between devices are 32-bit elements; how exact they have to be, the bound alone decides.
A program may use at most 192 MiB of HBM per device.

v0:
```python
import jax
import jax.numpy as jnp
from jax import lax
from jax.sharding import PartitionSpec as P

STEPS = 3


def from_root(array, axis, root):
    mine = lax.axis_index(axis) == root
    return lax.psum(jnp.where(mine, array, jnp.zeros_like(array)), axis)


def shifted(block, axis, distance):
    devices = range(lax.axis_size(axis))
    route = [((i - distance) % len(devices), i) for i in devices]
    return lax.ppermute(block, axis, route)


def padded(block, sides, width):
    for axis, dim in sides:
        count = lax.axis_size(axis)
        forward = [(i, i + 1) for i in range(count - 1)]
        forward.append((count - 1, 0))
        backward = [(target, source) for source, target in forward]
        low = lax.ppermute(
            lax.slice_in_dim(block, block.shape[dim] - width, None, axis=dim), axis, forward
        )
        high = lax.ppermute(lax.slice_in_dim(block, 0, width, axis=dim), axis, backward)
        block = jnp.concatenate([low, block, high], axis=dim)
    return block


def shift_prev(field, axis):
    first = jnp.zeros_like(lax.slice_in_dim(field, 0, 1, axis=axis))
    rest = lax.slice_in_dim(field, 0, field.shape[axis] - 1, axis=axis)
    return jnp.concatenate([first, rest], axis=axis)


def shift_next(field, axis):
    last = jnp.zeros_like(lax.slice_in_dim(field, 0, 1, axis=axis))
    rest = lax.slice_in_dim(field, 1, field.shape[axis], axis=axis)
    return jnp.concatenate([rest, last], axis=axis)


def column_update(adjoint, faces, axis):
    face_axis = faces.ndim - (adjoint.ndim - axis)
    outflow = jnp.maximum(faces, 0.0)
    inflow = shift_prev(jnp.minimum(faces, 0.0), face_axis)
    after_cell = shift_next(adjoint, axis)
    before_cell = shift_prev(adjoint, axis)
    return adjoint + outflow * (after_cell - adjoint) + inflow * (adjoint - before_cell)


def lon_update(widened, faces):
    centre = widened[:, :, 1:-1]
    after_cell = widened[:, :, 2:]
    before_cell = widened[:, :, :-2]
    outflow = jnp.maximum(faces[1:], 0.0)
    inflow = jnp.minimum(faces[:-1], 0.0)
    return centre + outflow * (after_cell - centre) + inflow * (centre - before_cell)


def inject(adjoint, cells, hours, values, turn_index, offset, region_cols, band_start, all_cols):
    plane_size = adjoint.shape[3] * adjoint.shape[4]
    base_column = jnp.remainder(cells // plane_size - band_start - offset, all_cols)
    flattened = adjoint.reshape(adjoint.shape[1], -1)
    column = base_column + 0
    active = (hours == turn_index) & (column < region_cols)
    target = jnp.where(active, column * plane_size + cells % plane_size, region_cols * plane_size)
    flattened = flattened.at[:, target].add(jnp.where(active, values, 0.0), mode="drop")
    return flattened.reshape(adjoint.shape)


def keep_masks(met_block):
    lat_keep = lax.broadcasted_iota(jnp.int32, met_block.shape[1:], 2) < met_block.shape[3] - 1
    lev_keep = lax.broadcasted_iota(jnp.int32, met_block.shape[1:], 1) < met_block.shape[2] - 1
    return (jnp.where(lat_keep, met_block[1], 0.0), jnp.where(lev_keep, met_block[2], 0.0))


def local(adjoint_in, courants, owner, rcpt_cell, rcpt_hour, forcing):
    band_cols = adjoint_in.shape[2]
    all_cols = band_cols * lax.axis_size("lon")
    band_start = lax.axis_index("lon") * band_cols
    cells = rcpt_cell[0]
    hours = rcpt_hour[0]
    values = forcing[0]
    own_slot = courants[0]
    met_block = from_root(own_slot, "rcpt", owner[0])
    adjoint = adjoint_in
    previous_edge = shifted(met_block[0][-1:], "lon", 1)
    east_faces = jnp.concatenate([previous_edge, met_block[0]], axis=0)
    north_faces, upper_faces = keep_masks(met_block)
    for turn_index in range(STEPS):
        adjoint = inject(
            adjoint, cells, hours, values, turn_index, 0, band_cols, band_start, all_cols
        )
        widened = padded(adjoint, (("lon", 2),), 1)
        adjoint = lon_update(widened, east_faces)
        adjoint = column_update(adjoint, north_faces, 4)
        adjoint = column_update(adjoint, upper_faces, 3)
    return adjoint


def solution(mesh):
    in_specs = (
        P("rcpt", None, "lon", None, None),
        P("rcpt", None, "lon", None, None),
        P("lon"),
        P("rcpt", None),
        P("rcpt", None),
        P("rcpt", None, None),
    )
    out_specs = P("rcpt", None, "lon", None, None)
    return jax.shard_map(local, mesh=mesh, in_specs=in_specs, out_specs=out_specs, check_vma=False)
```

profile of v0, /device:TPU:0, one launch (start us, length us, event | category | flops | bytes accessed | tf_op | source)
XLA Modules:
  0.0 231.6 jit_solution(17080490130106043624)
XLA Ops:
  6.5 0.8 compare_reduce_fusion
  7.3 0.7 compare_select_fusion
  8.1 0.7 fusion.34
  8.8 0.7 fusion.23
  9.7 9.7 %copy.34 = f32[1,4,16,16,128]{1,4,3,2,0:T(8,128)} copy(f32[1,4,16,16,128]{4,3,2,1,0:T(8,128)} %param.6) | data formatting | bytes 1048576 | tf_op args[0]
  19.4 14.5 %scatter_fusion = f32[4,32768]{0,1:T(8,128)} fusion(f32[4,32768]{0,1:T(8,128)} %bitcast.83, s32[512]{0:T(512)S(1)} %bitcast.90, f32[512,4]{1,0:T(8,128)S(1)} %copy.35), kind=kCustom, calls=%fused_computation | custom fusion | flops 2048 | bytes 26624 | tf_op jit(solution)/shard_map/scatter-add | solution.py:71
  33.9 10.0 %copy.39 = f32[1,4,16,16,128]{4,3,2,1,0:T(8,128)S(1)} copy(f32[1,4,16,16,128]{1,4,3,2,0:T(8,128)} %bitcast.84) | data formatting | bytes 1048576 | tf_op jit(solution)/shard_map/reshape | solution.py:72
  43.9 3.0 %collective-permute-start = (f32[1,4,1,16,128]{4,3,2,1,0:T(8,128)S(1)}, f32[1,4,1,16,128]{4,3,2,1,0:T(8,128)S(1)}, u32[]{:S(2)}, u32[]{:S(2)}) collective-permute-start(f32[1,4,1,16,128]{4,3,2,1,0:T(8,128)S(1)} %get-tuple-element.33), channel_id=1, source_target_pairs={{1,0},{0,1},{3,2},{2,3},{5,4},{4,5},{7,6},{6,7},{9,8},{8,9},{11,10... | collective-permute-start | bytes 98312 | tf_op jit(solution)/shard_map/ppermute | solution.py:29
  47.7 0.8 select_bitcast_fusion
  48.6 92.2 %all-reduce.16.cloned.1.call-done = f32[3,16,16,128]{3,2,1,0:T(8,128)} async-done(((f32[3,16,16,128]{3,2,1,0:T(8,128)}), f32[3,16,16,128]{3,2,1,0:T(8,128)}) %all-reduce.16.cloned.1.call-update) | async-done | bytes 393232 | tf_op jit(solution)/shard_map/psum | solution.py:11
  140.9 0.7 slice_bitcast_fusion.3
  141.6 1.5 collective-permute-start.1
  143.0 1.1 broadcast_maximum_fusion
  144.2 0.9 slice_bitcast_fusion.2
  145.6 0.3 multiply_add_fusion.5
  146.1 8.6 %copy.43 = f32[1,4,16,16,128]{1,4,3,2,0:T(8,128)} copy(f32[1,4,16,16,128]{4,3,2,1,0:T(8,128)S(1)} %multiply_add_fusion.4) | data formatting | bytes 1048576 | tf_op jit(solution)/shard_map/add | solution.py:52
  154.7 14.5 %scatter_fusion.1 = f32[4,32768]{0,1:T(8,128)} fusion(f32[4,32768]{0,1:T(8,128)} %bitcast.85, s32[512]{0:T(512)S(1)} %bitcast.89, f32[512,4]{1,0:T(8,128)S(1)} %copy.44), kind=kCustom, calls=%fused_computation.1 | custom fusion | flops 2048 | bytes 26624 | tf_op jit(solution)/shard_map/scatter-add | solution.py:71
  169.2 10.0 %copy.48 = f32[1,4,16,16,128]{4,3,2,1,0:T(8,128)S(1)} copy(f32[1,4,16,16,128]{1,4,3,2,0:T(8,128)} %bitcast.86) | data formatting | bytes 1048576 | tf_op jit(solution)/shard_map/reshape | solution.py:72
  179.2 1.5 collective-permute-start.3
  180.7 0.6 collective-permute-start.4
  181.5 1.7 collective-permute-done.3
  183.2 1.4 collective-permute-done.4
  184.9 0.3 multiply_add_fusion.3
  185.5 8.6 %copy.52 = f32[1,4,16,16,128]{1,4,3,2,0:T(8,128)} copy(f32[1,4,16,16,128]{4,3,2,1,0:T(8,128)S(1)} %multiply_add_fusion.2) | data formatting | bytes 1048576 | tf_op jit(solution)/shard_map/add | solution.py:52
  194.1 14.5 %scatter_fusion.2 = f32[4,32768]{0,1:T(8,128)} fusion(f32[4,32768]{0,1:T(8,128)} %bitcast.87, s32[512]{0:T(512)S(1)} %bitcast.91, f32[512,4]{1,0:T(8,128)S(1)} %copy.53), kind=kCustom, calls=%fused_computation.2 | custom fusion | flops 2048 | bytes 26624 | tf_op jit(solution)/shard_map/scatter-add | solution.py:71
  208.6 10.0 %copy.57 = f32[1,4,16,16,128]{4,3,2,1,0:T(8,128)S(1)} copy(f32[1,4,16,16,128]{1,4,3,2,0:T(8,128)} %bitcast.88) | data formatting | bytes 1048576 | tf_op jit(solution)/shard_map/reshape | solution.py:72
  218.6 0.7 collective-permute-start.5
  219.2 1.4 collective-permute-start.6
  220.7 1.9 collective-permute-done.5
  222.5 0.6 collective-permute-done.6
  223.4 0.3 multiply_add_fusion.1
  223.8 1.0 multiply_add_fusion
  (36 shorter events, 2.2 us)
Async XLA Ops:
  6.5 12.9 %copy-start.1 = (s32[1,512]{1,0:T(1,128)S(1)}, s32[1,512]{1,0:T(1,128)}, u32[]{:S(2)}) copy-start(s32[1,512]{1,0:T(1,128)} %param.10) | copy-start | bytes 6148
  6.5 134.3 %all-reduce.16.cloned.1.call-start = ((), (), s32[]{:S(2)}) async-start(), calls=%async_computation | async-start | bytes 786432 | tf_op jit(solution)/shard_map/psum | solution.py:11
  9.6 38.0 %copy-start = (f32[1,3,16,16,128]{4,3,2,1,0:T(8,128)S(1)}, f32[1,3,16,16,128]{4,3,2,1,0:T(8,128)}, u32[]{:S(2)}) copy-start(f32[1,3,16,16,128]{4,3,2,1,0:T(8,128)} %param.7) | copy-start | bytes 1179652
  43.9 101.4 %collective-permute-start = (f32[1,4,1,16,128]{4,3,2,1,0:T(8,128)S(1)}, f32[1,4,1,16,128]{4,3,2,1,0:T(8,128)S(1)}, u32[]{:S(2)}, u32[]{:S(2)}) collective-permute-start(f32[1,4,1,16,128]{4,3,2,1,0:T(8,128)S(1)} %get-tuple-element.33), channel_id=1, source_target_pairs={{1,0},{0,1},{3,2},{2,3},{5,4},{4,5},{7,6},{6,7},{9,8},{8,9},{11,10... | collective-permute-start | bytes 98312 | tf_op jit(solution)/shard_map/ppermute | solution.py:29
  46.9 98.4 %collective-permute-start.2 = (f32[1,4,1,16,128]{4,3,2,1,0:T(8,128)S(1)}, f32[1,4,1,16,128]{4,3,2,1,0:T(8,128)S(1)}, u32[]{:S(2)}, u32[]{:S(2)}) collective-permute-start(f32[1,4,1,16,128]{4,3,2,1,0:T(8,128)S(1)} %get-tuple-element.34), channel_id=1, source_target_pairs={{0,1},{1,0},{2,3},{3,2},{4,5},{5,4},{6,7},{7,6},{8,9},{9,8},{10,11... | collective-permute-start | bytes 98312 | tf_op jit(solution)/shard_map/ppermute | solution.py:26
  141.6 3.7 %collective-permute-start.1 = (f32[1,16,128]{2,1,0:T(8,128)S(1)}, f32[1,16,128]{2,1,0:T(8,128)S(1)}, u32[]{:S(2)}, u32[]{:S(2)}) collective-permute-start(f32[1,16,128]{2,1,0:T(8,128)S(1)} %slice_bitcast_fusion.3), channel_id=1, source_target_pairs={{1,0},{0,1},{3,2},{2,3},{5,4},{4,5},{7,6},{6,7},{9,8},{8,9},{11,10... | collective-permute-start | bytes 24584 | tf_op jit(solution)/shard_map/ppermute | solution.py:17
  179.2 4.0 %collective-permute-start.3 = (f32[1,4,1,16,128]{4,3,2,1,0:T(8,128)S(1)}, f32[1,4,1,16,128]{4,3,2,1,0:T(8,128)S(1)}, u32[]{:S(2)}, u32[]{:S(2)}) collective-permute-start(f32[1,4,1,16,128]{4,3,2,1,0:T(8,128)S(1)} %get-tuple-element.27), channel_id=1, source_target_pairs={{1,0},{0,1},{3,2},{2,3},{5,4},{4,5},{7,6},{6,7},{9,8},{8,9},{11,10... | collective-permute-start | bytes 98312 | tf_op jit(solution)/shard_map/ppermute | solution.py:29
  180.7 3.9 %collective-permute-start.4 = (f32[1,4,1,16,128]{4,3,2,1,0:T(8,128)S(1)}, f32[1,4,1,16,128]{4,3,2,1,0:T(8,128)S(1)}, u32[]{:S(2)}, u32[]{:S(2)}) collective-permute-start(f32[1,4,1,16,128]{4,3,2,1,0:T(8,128)S(1)} %get-tuple-element.28), channel_id=1, source_target_pairs={{0,1},{1,0},{2,3},{3,2},{4,5},{5,4},{6,7},{7,6},{8,9},{9,8},{10,11... | collective-permute-start | bytes 98312 | tf_op jit(solution)/shard_map/ppermute | solution.py:26
  218.6 4.0 %collective-permute-start.5 = (f32[1,4,1,16,128]{4,3,2,1,0:T(8,128)S(1)}, f32[1,4,1,16,128]{4,3,2,1,0:T(8,128)S(1)}, u32[]{:S(2)}, u32[]{:S(2)}) collective-permute-start(f32[1,4,1,16,128]{4,3,2,1,0:T(8,128)S(1)} %get-tuple-element.21), channel_id=1, source_target_pairs={{1,0},{0,1},{3,2},{2,3},{5,4},{4,5},{7,6},{6,7},{9,8},{8,9},{11,10... | collective-permute-start | bytes 98312 | tf_op jit(solution)/shard_map/ppermute | solution.py:29
  219.2 3.9 %collective-permute-start.6 = (f32[1,4,1,16,128]{4,3,2,1,0:T(8,128)S(1)}, f32[1,4,1,16,128]{4,3,2,1,0:T(8,128)S(1)}, u32[]{:S(2)}, u32[]{:S(2)}) collective-permute-start(f32[1,4,1,16,128]{4,3,2,1,0:T(8,128)S(1)} %get-tuple-element.22), channel_id=1, source_target_pairs={{0,1},{1,0},{2,3},{3,2},{4,5},{5,4},{6,7},{7,6},{8,9},{9,8},{10,11... | collective-permute-start | bytes 98312 | tf_op jit(solution)/shard_map/ppermute | solution.py:26
Sparse Core Ops, SparseCore 0:
  48.6 92.2 all-reduce.15
where the time goes:
time: 232 us
  waiting for transfers between devices  97.9 us (42%)
  local copies, waits for them, and re-layouts  60 us (26%)
  other arithmetic  50.7 us (22%)
  between operations  14.3 us (6%)
  starting transfers between devices  8.73 us (4%)
    psum x1, waiting for transfers between devices, from_root(): return lax.psum(jnp.where(mine, array, jnp.zeros_like(array)), axis)  92.2 us
    scatter-add x3, other arithmetic, inject(): flattened.at[:, target].add(jnp.where(active, values, 0.0), mode='drop')  43.4 us
    reshape x3, local copies, waits for them, and re-layouts, inject(): return flattened.reshape(adjoint.shape)  30 us
    add x2, local copies, waits for them, and re-layouts, column_update(): adjoint + outflow * (after_cell - adjoint)  17.2 us
    unnamed x5, local copies, waits for them, and re-layouts  9.74 us
    ppermute x3, starting transfers between devices, padded(): lax.ppermute(lax.slice_in_dim(block, 0, width, axis=dim), axis, backward)  5.16 us
  transfers between devices with their start and end apart: 8, of which 5 were waited for; matrix products, arithmetic and copies ran while one was open for 2% of the time, Pallas kernels for 0%

commit v1 on v0

v1 whole, which is shorter than its diff:
```python
import functools

import jax
import jax.numpy as jnp
from jax import lax
from jax.experimental import pallas as pl
from jax.experimental.pallas import tpu as pltpu
from jax.sharding import PartitionSpec as P

STEPS = 3
HALO = STEPS
PIECE = 2
MESH = pl.DeviceIdType.MESH


def kernel(
    dims,
    owner_ref,
    cell_ref,
    hour_ref,
    value_ref,
    adjoint_hbm,
    met_hbm,
    out_hbm,
    ping,
    pong,
    result,
    met,
    coef,
    force,
    got,
    mid,
    piece,
    local_sem,
    out_sem,
    halo_send,
    halo_recv,
    scatter_send,
    scatter_recv,
    mid_send,
    mid_recv,
    gather_send,
    gather_recv,
    edge_send,
    edge_recv,
):
    rows, bands, tracers, cols, lev, lat, recs = dims
    group = cols // PIECE
    groups = rows // group
    wide = cols + 2 * HALO
    row = lax.axis_index("rcpt")
    band = lax.axis_index("lon")
    block = row // group
    place = row % group
    base = block * group
    left = (band + bands - 1) % bands
    right = (band + 1) % bands

    local_adjoint = pltpu.make_async_copy(
        adjoint_hbm.at[0], ping.at[:, pl.ds(HALO, cols)], local_sem.at[0]
    )
    local_adjoint.start()
    local_piece = pltpu.make_async_copy(
        met_hbm.at[0, :, pl.ds(place * PIECE, PIECE)], got.at[place], local_sem.at[1]
    )
    local_piece.start()

    barrier = pltpu.get_barrier_semaphore()

    def greet(r, b):
        pl.semaphore_signal(barrier, inc=1, device_id=(r, b), device_id_type=MESH)

    greeted = 0
    for d in range(1, group):
        greet(base + (place + d) % group, band)
        greeted += 1
    for d in range(1, groups):
        greet(((block + d) % groups) * group + place, band)
        greeted += 1
    greet(row, left)
    greet(row, right)
    greeted += 2
    greet(base, right)
    greet(base + group - 1, left)
    greet(base + group - 2, left)
    sends_edges = (place == 0) | (place >= group - 2)
    pl.semaphore_wait(barrier, greeted + jnp.where(sends_edges, group, 0))

    def remote(src, dst, send, recv, r, b):
        return pltpu.make_async_remote_copy(
            src_ref=src,
            dst_ref=dst,
            send_sem=send,
            recv_sem=recv,
            device_id=(r, b),
            device_id_type=MESH,
        )

    scatter = []
    for d in range(1, group):
        to = (place + d) % group
        copy = remote(
            met_hbm.at[0, :, pl.ds(to * PIECE, PIECE)],
            got.at[place],
            scatter_send.at[to],
            scatter_recv.at[place],
            base + to,
            band,
        )
        copy.start()
        scatter.append(copy)
    to_right = remote(
        adjoint_hbm.at[0, :, pl.ds(cols - HALO, HALO)],
        ping.at[:, pl.ds(0, HALO)],
        halo_send.at[0],
        halo_recv.at[0],
        row,
        right,
    )
    to_right.start()
    to_left = remote(
        adjoint_hbm.at[0, :, pl.ds(0, HALO)],
        ping.at[:, pl.ds(HALO + cols, HALO)],
        halo_send.at[1],
        halo_recv.at[1],
        row,
        left,
    )
    to_left.start()

    with jax.named_scope("receptors"):
        plane_bits = (lev * lat).bit_length() - 1
        lat_bits = lat.bit_length() - 1
        cells = cell_ref[...]
        hours = hour_ref[...]
        column = jnp.right_shift(cells, plane_bits) - band * cols + HALO
        column = jnp.where(column < 0, column + bands * cols, column)
        column = jnp.where(column >= bands * cols, column - bands * cols, column)
        level = jnp.bitwise_and(jnp.right_shift(cells, lat_bits), lev - 1)
        plane = jnp.where(column < wide, column * lev + level, -1)
        at_lat = jnp.bitwise_and(cells, lat - 1)
        lat_hit = lax.broadcasted_iota(jnp.int32, (lat, recs), 0) == at_lat
        parts = []
        for t in range(tracers):
            value = value_ref[0, t : t + 1, :]
            high = value.astype(jnp.bfloat16).astype(jnp.float32)
            rest = value - high
            parts.append(
                (
                    jnp.where(lat_hit, high, 0.0).astype(jnp.bfloat16),
                    jnp.where(lat_hit, rest, 0.0).astype(jnp.bfloat16),
                )
            )
        planes = lax.broadcasted_iota(jnp.int32, (wide * lev, recs), 0)
        contract = (((1,), (1,)), ((), ()))
        for s in range(STEPS):
            key = jnp.where(hours == s, plane, -1)
            hit = jnp.where(planes == key, 1.0, 0.0).astype(jnp.bfloat16)
            for t in range(tracers):
                high, rest = parts[t]
                total = lax.dot_general(hit, high, contract, preferred_element_type=jnp.float32)
                total += lax.dot_general(hit, rest, contract, preferred_element_type=jnp.float32)
                force[s, t] = total.reshape(wide, lev, lat)

    local_piece.wait()
    for d in range(1, group):
        source = (place + group - d) % group
        remote(
            got.at[source], got.at[source], scatter_send.at[source], scatter_recv.at[source], row, right
        ).wait_recv()
    owner = owner_ref[0]
    mid[block] = got[owner % group]
    between = []
    for d in range(1, groups):
        to = (block + d) % groups
        copy = remote(
            mid.at[block], mid.at[block], mid_send.at[to], mid_recv.at[block], to * group + place, band
        )
        copy.start()
        between.append(copy)

    local_adjoint.wait()
    to_right.wait()
    to_left.wait()

    def first_force(j, carry):
        for t in range(tracers):
            ping[t, j] = ping[t, j] + force[0, t, j]
        return carry

    lax.fori_loop(0, wide, first_force, 0)

    for d in range(1, groups):
        source = (block + groups - d) % groups
        remote(
            mid.at[source], mid.at[source], mid_send.at[source], mid_recv.at[source], row, right
        ).wait_recv()
    chosen = mid[owner // group]
    piece[...] = chosen
    mine = met.at[:, pl.ds(HALO + place * PIECE, PIECE)]
    gather = []
    for d in range(1, group):
        to = (place + d) % group
        copy = remote(piece, mine, gather_send.at[to], gather_recv.at[place], base + to, band)
        copy.start()
        gather.append(copy)

    def edges(start):
        def each(src, dst, which, b):
            for q in range(group):
                copy = remote(src, dst, edge_send.at[q], edge_recv.at[which], base + q, b)
                copy.start() if start else copy.wait_send()

        @pl.when(place == 0)
        def _():
            each(piece, met.at[:, pl.ds(HALO + cols, PIECE)], 0, left)

        @pl.when(place == group - 1)
        def _():
            each(piece, met.at[:, pl.ds(HALO - PIECE, PIECE)], 1, right)

        @pl.when(place == group - 2)
        def _():
            each(
                piece.at[pl.ds(0, 1), pl.ds(PIECE - 1, 1)],
                met.at[pl.ds(0, 1), pl.ds(HALO - PIECE - 1, 1)],
                2,
                right,
            )

    edges(True)
    met[:, pl.ds(HALO + place * PIECE, PIECE)] = chosen
    for d in range(1, group):
        source = (place + group - d) % group
        into = met.at[:, pl.ds(HALO + source * PIECE, PIECE)]
        remote(piece, into, gather_send.at[source], gather_recv.at[source], row, right).wait_recv()
    into = met.at[:, pl.ds(HALO + cols, PIECE)]
    remote(piece, into, edge_send.at[0], edge_recv.at[0], row, right).wait_recv()
    into = met.at[:, pl.ds(HALO - PIECE, PIECE)]
    remote(piece, into, edge_send.at[0], edge_recv.at[1], row, right).wait_recv()
    into = met.at[pl.ds(0, 1), pl.ds(HALO - PIECE - 1, 1)]
    remote(
        piece.at[pl.ds(0, 1), pl.ds(PIECE - 1, 1)], into, edge_send.at[0], edge_recv.at[2], row, right
    ).wait_recv()

    lat_keep = lax.broadcasted_iota(jnp.int32, (lev, lat), 1) < lat - 1
    lev_keep = lax.broadcasted_iota(jnp.int32, (lev, lat), 0) < lev - 1

    def factors(j):
        out_east = jnp.maximum(met[0, j], 0.0)
        in_east = jnp.maximum(-met[0, j - 1], 0.0)
        north = jnp.where(lat_keep, met[1, j], 0.0)
        out_north = jnp.maximum(north, 0.0)
        in_north = pltpu.roll(jnp.maximum(-north, 0.0), 1, 1)
        upper = jnp.where(lev_keep, met[2, j], 0.0)
        out_upper = jnp.maximum(upper, 0.0)
        in_upper = pltpu.roll(jnp.maximum(-upper, 0.0), 1, 0)
        return (
            1.0 - out_east - in_east,
            out_east,
            in_east,
            1.0 - out_north - in_north,
            out_north,
            in_north,
            1.0 - out_upper - in_upper,
            out_upper,
            in_upper,
        )

    def advance(source, t, j, f):
        field = f[0] * source[t, j] + f[1] * source[t, j + 1] + f[2] * source[t, j - 1]
        field = f[3] * field + f[4] * pltpu.roll(field, lat - 1, 1) + f[5] * pltpu.roll(field, 1, 1)
        return f[6] * field + f[7] * pltpu.roll(field, lev - 1, 0) + f[8] * pltpu.roll(field, 1, 0)

    def step_first(j, carry):
        f = factors(j)
        for i in range(9):
            coef[j, i] = f[i]
        for t in range(tracers):
            pong[t, j] = advance(ping, t, j, f) + force[1, t, j]
        return carry

    def step_middle(j, carry):
        f = [coef[j, i] for i in range(9)]
        for t in range(tracers):
            ping[t, j] = advance(pong, t, j, f) + force[2, t, j]
        return carry

    def step_last(j, carry):
        f = [coef[j, i] for i in range(9)]
        for t in range(tracers):
            result[t, j - HALO] = advance(ping, t, j, f)
        return carry

    lax.fori_loop(1, wide - 1, step_first, 0)
    lax.fori_loop(2, wide - 2, step_middle, 0)
    cut = 4
    part = cols // cut
    stores = []
    for k in range(cut):
        lax.fori_loop(HALO + k * part, HALO + (k + 1) * part, step_last, 0)
        store = pltpu.make_async_copy(
            result.at[:, pl.ds(k * part, part)], out_hbm.at[0, :, pl.ds(k * part, part)], out_sem.at[k]
        )
        store.start()
        stores.append(store)
    for copy in scatter + between + gather:
        copy.wait_send()
    edges(False)
    for store in stores:
        store.wait()


def local(adjoint_in, courants, owner, rcpt_cell, rcpt_hour, forcing):
    rows, bands = lax.axis_size("rcpt"), lax.axis_size("lon")
    _, tracers, cols, lev, lat = adjoint_in.shape
    recs = rcpt_cell.shape[1]
    group = cols // PIECE
    groups = rows // group
    wide = cols + 2 * HALO
    f32 = jnp.float32
    dma = pltpu.SemaphoreType.DMA
    vmem = pl.BlockSpec(memory_space=pltpu.VMEM)
    hbm = pl.BlockSpec(memory_space=pl.ANY)
    return pl.pallas_call(
        functools.partial(kernel, (rows, bands, tracers, cols, lev, lat, recs)),
        out_shape=jax.ShapeDtypeStruct(adjoint_in.shape, f32),
        in_specs=[pl.BlockSpec(memory_space=pltpu.SMEM), vmem, vmem, vmem, hbm, hbm],
        out_specs=hbm,
        scratch_shapes=[
            pltpu.VMEM((tracers, wide, lev, lat), f32),
            pltpu.VMEM((tracers, wide, lev, lat), f32),
            pltpu.VMEM((tracers, cols, lev, lat), f32),
            pltpu.VMEM((3, wide, lev, lat), f32),
            pltpu.VMEM((wide, 9, lev, lat), f32),
            pltpu.VMEM((STEPS, tracers, wide, lev, lat), f32),
            pltpu.VMEM((group, 3, PIECE, lev, lat), f32),
            pltpu.VMEM((groups, 3, PIECE, lev, lat), f32),
            pltpu.VMEM((3, PIECE, lev, lat), f32),
            dma((2,)),
            dma((4,)),
            dma((2,)),
            dma((2,)),
            dma((group,)),
            dma((group,)),
            dma((groups,)),
            dma((groups,)),
            dma((group,)),
            dma((group,)),
            dma((group,)),
            dma((3,)),
        ],
        compiler_params=pltpu.CompilerParams(
            collective_id=0, has_side_effects=True, vmem_limit_bytes=32 * 1024 * 1024
        ),
        cost_estimate=pl.CostEstimate(
            flops=2_300_000_000, bytes_accessed=1_500_000, transcendentals=0
        ),
    )(owner, rcpt_cell, rcpt_hour, forcing, adjoint_in, courants)


def solution(mesh):
    in_specs = (
        P("rcpt", None, "lon", None, None),
        P("rcpt", None, "lon", None, None),
        P("lon"),
        P("rcpt", None),
        P("rcpt", None),
        P("rcpt", None, None),
    )
    out_specs = P("rcpt", None, "lon", None, None)
    return jax.shard_map(local, mesh=mesh, in_specs=in_specs, out_specs=out_specs, check_vma=False)
```

time: 232 us -> 35.6 us (0.15)
  waiting for transfers between devices: 97.9 us -> 0 us
  local copies, waits for them, and re-layouts: 60 us -> 4.88 us
  other arithmetic: 50.7 us -> 0 us
  Pallas kernels: 0 us -> 29.7 us
  between operations: 14.3 us -> 0.67 us
  starting transfers between devices: 8.73 us -> 0 us
    psum x1 -> x0, waiting for transfers between devices: 92.2 us -> none  [from_root(): return lax.psum(jnp.where(mine, array, jnp.zeros_like(array)), axis)]
    scatter-add x3 -> x0, other arithmetic: 43.4 us -> none  [inject(): flattened.at[:, target].add(jnp.where(active, values, 0.0), mode='drop')]
    reshape x3 -> x0, local copies, waits for them, and re-layouts: 30 us -> none  [inject(): return flattened.reshape(adjoint.shape)]
    pallas_call x0 -> x1, Pallas kernels: none -> 29.7 us  [local(): pl.pallas_call(functools.partial(kernel, (rows, bands, tracers, cols, lev...]
    add x2 -> x0, local copies, waits for them, and re-layouts: 17.2 us -> none  [column_update(): adjoint + outflow * (after_cell - adjoint)]
    ppermute x7 -> x0, starting transfers between devices: 8.73 us -> none  [the longest x3 5.16 us: padded(): lax.ppermute(lax.slice_in_dim(block, 0, width, axis=dim), axis, backward)]
    ppermute x7 -> x0, waiting for transfers between devices: 5.66 us -> none  [the longest x3 3.63 us: padded(): lax.ppermute(lax.slice_in_dim(block, 0, width, axis=dim), axis, backward)]
    unnamed x5 -> x11, local copies, waits for them, and re-layouts: 9.74 us -> 4.88 us
  transfers between devices with their start and end apart: 8 -> 0, of which waited for: 5 -> 0; matrix products, arithmetic and copies ran while one was open for 2% -> 0% of each run, Pallas kernels for 0% -> 0%
where the time goes in v1:
time: 35.6 us; the launch traced here: 35.3 us
  Pallas kernels  29.7 us (83%)
  local copies, waits for them, and re-layouts  4.88 us (14%)
  between operations  0.67 us (2%)
    pallas_call x1, Pallas kernels, local(): pl.pallas_call(functools.partial(kernel, (rows, bands, tracers, cols, lev...  29.7 us
    unnamed x11, local copies, waits for them, and re-layouts  4.88 us

profile of v1, /device:TPU:0, one launch (start us, length us, event | category | flops | bytes accessed | tf_op | source)
XLA Modules:
  0.0 35.3 jit_solution(14850240715653804076)
XLA Ops:
  0.7 0.0 copy-start
  0.7 1.0 %copy-done = f32[1,4,16,16,128]{4,3,2,1,0:T(8,128)S(1)} copy-done((f32[1,4,16,16,128]{4,3,2,1,0:T(8,128)S(1)}, f32[1,4,16,16,128]{4,3,2,1,0:T(8,128)}, u32[]{:S(2)}) %copy-start) | copy-done | bytes 524312
  1.7 0.0 copy-start.1
  1.7 1.0 %copy-done.1 = f32[1,3,16,16,128]{4,3,2,1,0:T(8,128)S(1)} copy-done((f32[1,3,16,16,128]{4,3,2,1,0:T(8,128)S(1)}, f32[1,3,16,16,128]{4,3,2,1,0:T(8,128)}, u32[]{:S(2)}) %copy-start.1) | copy-done | bytes 393240
  2.7 0.0 copy-start.2
  2.7 0.7 %copy-done.2 = f32[1,4,512]{2,1,0:T(4,128)S(1)} copy-done((f32[1,4,512]{2,1,0:T(4,128)S(1)}, f32[1,4,512]{2,1,0:T(4,128)}, u32[]{:S(2)}) %copy-start.2) | copy-done | bytes 8216
  3.4 0.0 copy-start.3
  3.4 0.7 %copy-done.3 = s32[1,512]{1,0:T(1,128)S(1)} copy-done((s32[1,512]{1,0:T(1,128)S(1)}, s32[1,512]{1,0:T(1,128)}, u32[]{:S(2)}) %copy-start.3) | copy-done | bytes 2072
  4.1 0.0 copy-start.4
  4.1 0.7 %copy-done.4 = s32[1,512]{1,0:T(1,128)S(1)} copy-done((s32[1,512]{1,0:T(1,128)S(1)}, s32[1,512]{1,0:T(1,128)}, u32[]{:S(2)}) %copy-start.4) | copy-done | bytes 2072
  4.8 29.7 %shard_map.64 = f32[1,4,16,16,128]{4,3,2,1,0:T(8,128)S(1)} custom-call(s32[1]{0:T(128)S(6)} %copy.8.owner_ref, s32[1,512]{1,0:T(1,128)S(1)} %copy-done.3, s32[1,512]{1,0:T(1,128)S(1)} %copy-done.4, f32[1,4,512]{2,1,0:T(4,128)S(1)} %copy-done.2, f32[1,4,16,16,128]{4,3,2,1,0:T(8,128)S(1)} %copy-done, f32[1,3,16,16,128]{4,3,2,1,0:T(8,128)S(1)} %copy-done.1), custom_call_target="tpu_custom_call" | custom-call | flops 2300000000 | bytes 1500000 | tf_op jit(solution)/shard_map/pallas_call | solution.py:325
  34.5 0.8 %copy.9 = f32[1,4,16,16,128]{4,3,2,1,0:T(8,128)} copy(f32[1,4,16,16,128]{4,3,2,1,0:T(8,128)S(1)} %shard_map.64) | data formatting | bytes 1048576
Async XLA Ops:
  0.7 1.0 %copy-start = (f32[1,4,16,16,128]{4,3,2,1,0:T(8,128)S(1)}, f32[1,4,16,16,128]{4,3,2,1,0:T(8,128)}, u32[]{:S(2)}) copy-start(f32[1,4,16,16,128]{4,3,2,1,0:T(8,128)} %adjoint_hbm.1) | copy-start | bytes 1572868
  1.7 1.0 %copy-start.1 = (f32[1,3,16,16,128]{4,3,2,1,0:T(8,128)S(1)}, f32[1,3,16,16,128]{4,3,2,1,0:T(8,128)}, u32[]{:S(2)}) copy-start(f32[1,3,16,16,128]{4,3,2,1,0:T(8,128)} %met_hbm.1) | copy-start | bytes 1179652
  2.7 0.7 %copy-start.2 = (f32[1,4,512]{2,1,0:T(4,128)S(1)}, f32[1,4,512]{2,1,0:T(4,128)}, u32[]{:S(2)}) copy-start(f32[1,4,512]{2,1,0:T(4,128)} %value_ref.1) | copy-start | bytes 24580
  3.4 0.7 %copy-start.3 = (s32[1,512]{1,0:T(1,128)S(1)}, s32[1,512]{1,0:T(1,128)}, u32[]{:S(2)}) copy-start(s32[1,512]{1,0:T(1,128)} %cell_ref.1) | copy-start | bytes 6148
  4.1 0.7 %copy-start.4 = (s32[1,512]{1,0:T(1,128)S(1)}, s32[1,512]{1,0:T(1,128)}, u32[]{:S(2)}) copy-start(s32[1,512]{1,0:T(1,128)} %hour_ref.1) | copy-start | bytes 6148

commit v2 on v1

v2 whole, which is shorter than its diff:
```python
import functools

import jax
import jax.numpy as jnp
from jax import lax
from jax.experimental import pallas as pl
from jax.experimental.pallas import tpu as pltpu
from jax.sharding import PartitionSpec as P

STEPS = 3
HALO = STEPS
PIECE = 2
MESH = pl.DeviceIdType.MESH


def kernel(
    dims,
    owner_hbm,
    cell_hbm,
    hour_hbm,
    value_hbm,
    adjoint_hbm,
    met_hbm,
    out_hbm,
    owner_ref,
    cell_ref,
    hour_ref,
    value_ref,
    ping,
    pong,
    result,
    met,
    coef,
    force,
    got_even,
    got_odd,
    mid_even,
    mid_odd,
    piece,
    local_sem,
    out_sem,
    halo_send,
    halo_recv,
    scatter_send,
    scatter_recv,
    mid_send,
    mid_recv,
    gather_send,
    gather_recv,
    edge_send,
    edge_recv,
):
    rows, bands, tracers, cols, lev, lat, recs = dims
    got, mid = (got_even, got_odd), (mid_even, mid_odd)
    group = cols // PIECE
    groups = rows // group
    wide = cols + 2 * HALO
    row = lax.axis_index("rcpt")
    band = lax.axis_index("lon")
    block = row // group
    place = row % group
    base = block * group
    left = (band + bands - 1) % bands
    right = (band + 1) % bands

    barrier = pltpu.get_barrier_semaphore()

    def greet(r, b):
        pl.semaphore_signal(barrier, inc=1, device_id=(r, b), device_id_type=MESH)

    for d in range(1, group):
        greet(base + (place + d) % group, band)
    for d in range(1, groups):
        greet(((block + d) % groups) * group + place, band)
    greet(row, left)
    greet(row, right)

    def fetch(src, dst, which):
        copy = pltpu.make_async_copy(src, dst, local_sem.at[which])
        copy.start()
        return copy

    records = [
        fetch(cell_hbm, cell_ref, 0),
        fetch(hour_hbm, hour_ref, 1),
        fetch(value_hbm, value_ref, 2),
    ]
    own = [
        fetch(met_hbm.at[0, :, place * PIECE + k], got[k].at[place], 3 + k) for k in range(PIECE)
    ]
    own_owner = fetch(owner_hbm, owner_ref, 3 + PIECE)
    local_adjoint = fetch(adjoint_hbm.at[0], ping.at[:, pl.ds(HALO, cols)], 4 + PIECE)

    pl.semaphore_wait(barrier, group + groups)

    def remote(src, dst, send, recv, r, b):
        return pltpu.make_async_remote_copy(
            src_ref=src,
            dst_ref=dst,
            send_sem=send,
            recv_sem=recv,
            device_id=(r, b),
            device_id_type=MESH,
        )

    sent = []

    def send(*what):
        copy = remote(*what)
        copy.start()
        sent.append(copy)
        return copy

    for k in range(PIECE):
        for d in range(1, group):
            to = (place + d) % group
            send(
                met_hbm.at[0, :, to * PIECE + k],
                got[k].at[place],
                scatter_send.at[k, to],
                scatter_recv.at[k, place],
                base + to,
                band,
            )
    to_right = send(
        adjoint_hbm.at[0, :, pl.ds(cols - HALO, HALO)],
        ping.at[:, pl.ds(0, HALO)],
        halo_send.at[0],
        halo_recv.at[0],
        row,
        right,
    )
    to_left = send(
        adjoint_hbm.at[0, :, pl.ds(0, HALO)],
        ping.at[:, pl.ds(HALO + cols, HALO)],
        halo_send.at[1],
        halo_recv.at[1],
        row,
        left,
    )

    for copy in records:
        copy.wait()
    with jax.named_scope("receptors"):
        plane_bits = (lev * lat).bit_length() - 1
        lat_bits = lat.bit_length() - 1
        cells = cell_ref[...]
        hours = hour_ref[...]
        column = jnp.right_shift(cells, plane_bits) - band * cols + HALO
        column = jnp.where(column < 0, column + bands * cols, column)
        column = jnp.where(column >= bands * cols, column - bands * cols, column)
        level = jnp.bitwise_and(jnp.right_shift(cells, lat_bits), lev - 1)
        plane = jnp.where(column < wide, column * lev + level, -1)
        at_lat = jnp.bitwise_and(cells, lat - 1)
        lat_hit = lax.broadcasted_iota(jnp.int32, (lat, recs), 0) == at_lat
        parts = []
        for t in range(tracers):
            value = value_ref[0, t : t + 1, :]
            high = value.astype(jnp.bfloat16).astype(jnp.float32)
            rest = value - high
            parts.append(
                (
                    jnp.where(lat_hit, high, 0.0).astype(jnp.bfloat16),
                    jnp.where(lat_hit, rest, 0.0).astype(jnp.bfloat16),
                )
            )
        planes = lax.broadcasted_iota(jnp.int32, (wide * lev, recs), 0)
        contract = (((1,), (1,)), ((), ()))

    def inject(s):
        with jax.named_scope("receptors"):
            key = jnp.where(hours == s, plane, -1)
            hit = jnp.where(planes == key, 1.0, 0.0).astype(jnp.bfloat16)
            for t in range(tracers):
                high, rest = parts[t]
                total = lax.dot_general(hit, high, contract, preferred_element_type=jnp.float32)
                total += lax.dot_general(hit, rest, contract, preferred_element_type=jnp.float32)
                force[s, t] = total.reshape(wide, lev, lat)

    inject(0)

    own_owner.wait()
    owner = owner_ref[0]
    for k in range(PIECE):
        own[k].wait()
        for d in range(1, group):
            source = (place + group - d) % group
            into = got[k].at[source]
            remote(
                into, into, scatter_send.at[k, source], scatter_recv.at[k, source], row, right
            ).wait_recv()
        mid[k][block] = got[k][owner % group]
        for d in range(1, groups):
            to = (block + d) % groups
            send(
                mid[k].at[block],
                mid[k].at[block],
                mid_send.at[k, to],
                mid_recv.at[k, block],
                to * group + place,
                band,
            )
    inject(1)

    for k in range(PIECE):
        for d in range(1, groups):
            source = (block + groups - d) % groups
            into = mid[k].at[source]
            remote(into, into, mid_send.at[k, source], mid_recv.at[k, source], row, right).wait_recv()
        chosen = mid[k][owner // group]
        piece[k] = chosen
        mine = HALO + place * PIECE + k
        for d in range(1, group):
            to = (place + d) % group
            send(
                piece.at[k], met.at[:, mine], gather_send.at[k, to], gather_recv.at[k, place], base + to, band
            )
        met[:, mine] = chosen
    for s in range(2, STEPS):
        inject(s)

    local_adjoint.wait()
    to_right.wait_recv()
    to_left.wait_recv()

    def first_force(j, carry):
        for t in range(tracers):
            ping[t, j] = ping[t, j] + force[0, t, j]
        return carry

    lax.fori_loop(0, wide, first_force, 0)

    def arrive(q):
        @pl.when(place != q)
        def _():
            for k in range(PIECE):
                into = met.at[:, HALO + q * PIECE + k]
                remote(
                    piece.at[k], into, gather_send.at[k, q], gather_recv.at[k, q], row, right
                ).wait_recv()

    for q in (0, group - 2, group - 1):
        arrive(q)
    last = HALO + cols
    edges = [
        send(
            met.at[:, pl.ds(HALO, PIECE)],
            met.at[:, pl.ds(last, PIECE)],
            edge_send.at[0],
            edge_recv.at[0],
            row,
            left,
        ),
        send(
            met.at[:, pl.ds(last - PIECE, PIECE)],
            met.at[:, pl.ds(HALO - PIECE, PIECE)],
            edge_send.at[1],
            edge_recv.at[1],
            row,
            right,
        ),
        send(
            met.at[0, last - HALO],
            met.at[0, 0],
            edge_send.at[2],
            edge_recv.at[2],
            row,
            right,
        ),
    ]
    for q in range(1, group - 2):
        arrive(q)

    lat_keep = lax.broadcasted_iota(jnp.int32, (lev, lat), 1) < lat - 1
    lev_keep = lax.broadcasted_iota(jnp.int32, (lev, lat), 0) < lev - 1

    def factors(j):
        out_east = jnp.maximum(met[0, j], 0.0)
        in_east = jnp.maximum(-met[0, j - 1], 0.0)
        north = jnp.where(lat_keep, met[1, j], 0.0)
        out_north = jnp.maximum(north, 0.0)
        in_north = pltpu.roll(jnp.maximum(-north, 0.0), 1, 1)
        upper = jnp.where(lev_keep, met[2, j], 0.0)
        out_upper = jnp.maximum(upper, 0.0)
        in_upper = pltpu.roll(jnp.maximum(-upper, 0.0), 1, 0)
        return (
            1.0 - out_east - in_east,
            out_east,
            in_east,
            1.0 - out_north - in_north,
            out_north,
            in_north,
            1.0 - out_upper - in_upper,
            out_upper,
            in_upper,
        )

    def advance(source, t, j, f):
        field = f[0] * source[t, j] + f[1] * source[t, j + 1] + f[2] * source[t, j - 1]
        field = f[3] * field + f[4] * pltpu.roll(field, lat - 1, 1) + f[5] * pltpu.roll(field, 1, 1)
        return f[6] * field + f[7] * pltpu.roll(field, lev - 1, 0) + f[8] * pltpu.roll(field, 1, 0)

    def step_first(j, carry):
        f = factors(j)
        for i in range(9):
            coef[j, i] = f[i]
        for t in range(tracers):
            pong[t, j] = advance(ping, t, j, f) + force[1, t, j]
        return carry

    def step_middle(j, carry):
        f = [coef[j, i] for i in range(9)]
        for t in range(tracers):
            ping[t, j] = advance(pong, t, j, f) + force[2, t, j]
        return carry

    def step_last(j, carry):
        f = [coef[j, i] for i in range(9)]
        for t in range(tracers):
            result[t, j - HALO] = advance(ping, t, j, f)
        return carry

    def store(first, count, which):
        copy = pltpu.make_async_copy(
            result.at[:, pl.ds(first, count)], out_hbm.at[0, :, pl.ds(first, count)], out_sem.at[which]
        )
        copy.start()
        return copy

    low, high = HALO + 1, last
    for body in (step_first, step_middle, step_last):
        lax.fori_loop(low, high, body, 0, unroll=2)
        low, high = low + 1, high - 1
    inner = store(HALO, cols - 2 * HALO + 1, 0)
    for edge in edges:
        edge.wait_recv()
    low, high = HALO + 1, last
    for s, body in enumerate((step_first, step_middle, step_last)):
        lax.fori_loop(s + 1, low, body, 0, unroll=2)
        lax.fori_loop(high, wide - 1 - s, body, 0, unroll=2)
        low, high = low + 1, high - 1
    stores = [inner, store(0, HALO, 1), store(cols - HALO + 1, HALO - 1, 2)]
    for copy in sent:
        copy.wait_send()
    for copy in stores:
        copy.wait()


def local(adjoint_in, courants, owner, rcpt_cell, rcpt_hour, forcing):
    rows, bands = lax.axis_size("rcpt"), lax.axis_size("lon")
    _, tracers, cols, lev, lat = adjoint_in.shape
    recs = rcpt_cell.shape[1]
    group = cols // PIECE
    groups = rows // group
    wide = cols + 2 * HALO
    f32 = jnp.float32
    dma = pltpu.SemaphoreType.DMA
    hbm = pl.BlockSpec(memory_space=pltpu.HBM)
    return pl.pallas_call(
        functools.partial(kernel, (rows, bands, tracers, cols, lev, lat, recs)),
        out_shape=jax.ShapeDtypeStruct(adjoint_in.shape, f32),
        in_specs=[hbm] * 6,
        out_specs=hbm,
        scratch_shapes=[
            pltpu.SMEM((1,), jnp.int32),
            pltpu.VMEM((1, recs), jnp.int32),
            pltpu.VMEM((1, recs), jnp.int32),
            pltpu.VMEM((1, tracers, recs), f32),
            pltpu.VMEM((tracers, wide, lev, lat), f32),
            pltpu.VMEM((tracers, wide, lev, lat), f32),
            pltpu.VMEM((tracers, cols, lev, lat), f32),
            pltpu.VMEM((3, wide, lev, lat), f32),
            pltpu.VMEM((wide, 9, lev, lat), f32),
            pltpu.VMEM((STEPS, tracers, wide, lev, lat), f32),
            pltpu.VMEM((group, 3, lev, lat), f32),
            pltpu.VMEM((group, 3, lev, lat), f32),
            pltpu.VMEM((groups, 3, lev, lat), f32),
            pltpu.VMEM((groups, 3, lev, lat), f32),
            pltpu.VMEM((PIECE, 3, lev, lat), f32),
            dma((5 + PIECE,)),
            dma((3,)),
            dma((2,)),
            dma((2,)),
            dma((PIECE, group)),
            dma((PIECE, group)),
            dma((PIECE, groups)),
            dma((PIECE, groups)),
            dma((PIECE, group)),
            dma((PIECE, group)),
            dma((3,)),
            dma((3,)),
        ],
        compiler_params=pltpu.CompilerParams(
            collective_id=0, has_side_effects=True, vmem_limit_bytes=60 * 1024 * 1024
        ),
        cost_estimate=pl.CostEstimate(
            flops=2_300_000_000, bytes_accessed=1_500_000, transcendentals=0
        ),
    )(owner, rcpt_cell, rcpt_hour, forcing, adjoint_in, courants)


def solution(mesh):
    in_specs = (
        P("rcpt", None, "lon", None, None),
        P("rcpt", None, "lon", None, None),
        P("lon"),
        P("rcpt", None),
        P("rcpt", None),
        P("rcpt", None, None),
    )
    out_specs = P("rcpt", None, "lon", None, None)
    return jax.shard_map(local, mesh=mesh, in_specs=in_specs, out_specs=out_specs, check_vma=False)
```

time: 35.6 us -> 28.6 us (0.80)
  Pallas kernels: 29.7 us -> 25.9 us
  local copies, waits for them, and re-layouts: 4.88 us -> 1.87 us
    pallas_call x1, Pallas kernels: 29.7 us -> 25.9 us  [local(): pl.pallas_call(functools.partial(kernel, (rows, bands, tracers, cols, lev...]
    unnamed x11 -> x1, local copies, waits for them, and re-layouts: 4.88 us -> 1.87 us
where the time goes in v2:
time: 28.6 us; the launch traced here: 28.5 us
  Pallas kernels  25.9 us (91%)
  local copies, waits for them, and re-layouts  1.87 us (7%)
  between operations  0.66 us (2%)
    pallas_call x1, Pallas kernels, local(): pl.pallas_call(functools.partial(kernel, (rows, bands, tracers, cols, lev...  25.9 us
    unnamed x1, local copies, waits for them, and re-layouts  1.87 us

profile of v2, /device:TPU:0, one launch (start us, length us, event | category | flops | bytes accessed | tf_op | source)
XLA Modules:
  0.0 28.5 jit_solution(17947396655455634287)
XLA Ops:
  0.7 25.9 %shard_map.64 = f32[1,4,16,16,128]{4,3,2,1,0:T(8,128)} custom-call(s32[1]{0:T(128)S(6)} %copy.8.owner_hbm, s32[1,512]{1,0:T(1,128)} %cell_hbm.1, s32[1,512]{1,0:T(1,128)} %hour_hbm.1, f32[1,4,512]{2,1,0:T(4,128)} %value_hbm.1, f32[1,4,16,16,128]{4,3,2,1,0:T(8,128)} %adjoint_hbm.1, f32[1,3,16,16,128]{4,3,2,1,0:T(8,128)} %met_hbm.1), custom_call_target="tpu_custom_call" | custom-call | flops 2300000000 | bytes 1500000 | tf_op jit(solution)/shard_map/pallas_call | solution.py:359
  26.6 1.9 %copy.9 = f32[1,4,16,16,128]{4,3,2,1,0:T(8,128)} copy(f32[1,4,16,16,128]{4,3,2,1,0:T(8,128)} %shard_map.64) | data formatting | bytes 1048576

commit v3 on v2

--- a/solution.py
+++ b/solution.py
@@ -317,7 +317,7 @@
     def step_last(j, carry):
         f = [coef[j, i] for i in range(9)]
         for t in range(tracers):
-            result[t, j - HALO] = advance(ping, t, j, f)
+            result[t, j - HALO] = -advance(ping, t, j, f)
         return carry
 
     def store(first, count, which):
@@ -356,7 +356,7 @@
     f32 = jnp.float32
     dma = pltpu.SemaphoreType.DMA
     hbm = pl.BlockSpec(memory_space=pltpu.HBM)
-    return pl.pallas_call(
+    return -pl.pallas_call(
         functools.partial(kernel, (rows, bands, tracers, cols, lev, lat, recs)),
         out_shape=jax.ShapeDtypeStruct(adjoint_in.shape, f32),
         in_specs=[hbm] * 6,

time: 28.6 us -> 28.6 us (level)
  other arithmetic: 0 us -> 1.87 us
  local copies, waits for them, and re-layouts: 1.87 us -> 0 us
    neg x0 -> x1, other arithmetic: none -> 1.87 us  [local(): -pl.pallas_call(functools.partial(kernel, (rows, bands, tracers, cols, le...]
    unnamed x1 -> x0, local copies, waits for them, and re-layouts: 1.87 us -> none
where the time goes in v3:
time: 28.6 us; the launch traced here: 28.5 us
  Pallas kernels  25.9 us (91%)
  other arithmetic  1.87 us (7%)
  between operations  0.66 us (2%)
    pallas_call x1, Pallas kernels, local(): pl.pallas_call(functools.partial(kernel, (rows, bands, tracers, cols, lev...  25.9 us
    neg x1, other arithmetic, local(): -pl.pallas_call(functools.partial(kernel, (rows, bands, tracers, cols, le...  1.87 us

profile of v3, /device:TPU:0, one launch (start us, length us, event | category | flops | bytes accessed | tf_op | source)
XLA Modules:
  0.0 28.5 jit_solution(88131881875169006)
XLA Ops:
  0.7 25.9 %shard_map.64 = f32[1,4,16,16,128]{4,3,2,1,0:T(8,128)} custom-call(s32[1]{0:T(128)S(6)} %copy.7.owner_hbm, s32[1,512]{1,0:T(1,128)} %cell_hbm.1, s32[1,512]{1,0:T(1,128)} %hour_hbm.1, f32[1,4,512]{2,1,0:T(4,128)} %value_hbm.1, f32[1,4,16,16,128]{4,3,2,1,0:T(8,128)} %adjoint_hbm.1, f32[1,3,16,16,128]{4,3,2,1,0:T(8,128)} %met_hbm.1), custom_call_target="tpu_custom_call" | custom-call | flops 2300000000 | bytes 1500000 | tf_op jit(solution)/shard_map/pallas_call | solution.py:359
  26.6 1.9 %neg.3 = f32[1,4,16,16,128]{4,3,2,1,0:T(8,128)} negate(f32[1,4,16,16,128]{4,3,2,1,0:T(8,128)} %shard_map.64) | non-fusion elementwise | flops 131072 | bytes 1048576 | tf_op jit(solution)/shard_map/neg | solution.py:359
